TPU v7x, 512 devices: a whole 4x8x8 slice. The times are simulated.
512 devices in a mesh: energy: 8 (over x, core), space: 64 (over y, z).
Axes of the slice: x: 4, y: 8, z: 8, core: 2. Of those that a mesh axis runs over, the one named last changes fastest.
Arguments:
- green_blocks: bfloat16 [16, 64, 256, 256], P('energy', 'space'), as said below
- energy_weights: float32 [16], P('energy'), may hold values from 0.00625 to 0.0625
- basis: bfloat16 [64, 256, 64, 256], P('space', None, 'energy'), may hold values from -0.75 to 0.75
- block_layer: int32 [64], P('space'), may hold values from 0 to 255, as said below
- potential_in: float32 [256, 64, 256], P('space', 'energy'), may hold values from -6 to 6
- doping: float32 [256, 64, 256], P('space', 'energy'), may hold values from -12 to 12
Outputs:
- potential: float32 [256, 64, 256], P('space', 'energy')
- residual: float32 [256, 64, 256], P('space', 'energy')
- onsite: float32 [64, 256], P('space')
Inputs may be any that keep to these rules, and one draw needn't show every extreme that they name: `green_blocks`: each block G[e, b] is symmetric positive definite. `block_layer`: block b lies in the slab of the space index that holds it or in the next slab: its layer is at least (b) * 4 and under (b + 2) * 4; the first block takes layer 0 and the last takes layer 255.
All inputs are finite; a program needn't handle non-finite values.
Results may differ from a plain program's by a relative error of at most 0.0035.
Values may be sent and summed in bfloat16 or wider, within the bound.
No kernel may reach another device: no remote copies, remote signals or barrier semaphores. Data moves between devices by JAX's collectives and lax.ppermute only.
A program may use at most 64 MiB of HBM per device.

v0:
```python
import jax
import jax.numpy as jnp
from jax import lax
from jax.experimental import pallas as pl
from jax.experimental.pallas import tpu as pltpu
from jax.sharding import PartitionSpec as P

ITERS = 3
HALO = 3
F32 = jnp.float32
BF16 = jnp.bfloat16


def moved(value, axis, by):
    count = lax.axis_size(axis)
    pairs = [(i, i + by) for i in range(count) if 0 <= i + by < count]
    return lax.ppermute(value, axis, pairs)


def along_z(field):
    zero = jnp.zeros_like(field[..., :1])
    up = jnp.concatenate([field[..., 1:], zero], axis=-1)
    down = jnp.concatenate([zero, field[..., :-1]], axis=-1)
    return up + down


def neighbours_in_block(field):
    total = along_z(field)
    for dim in (0, 1):
        width = [(0, 0)] * 3
        width[dim] = (1, 1)
        padded = jnp.pad(field, width)
        count = field.shape[dim]
        total = total + lax.slice_in_dim(padded, 0, count, axis=dim)
        total = total + lax.slice_in_dim(padded, 2, count + 2, axis=dim)
    return total


def coefficients(m):
    gaps = [a - b for a, b in zip(m, m[1:])]

    def norm_of(a, weights):
        total = 0.0
        for i, x in enumerate(a):
            total = total + x * x * weights[2 * i]
            for j in range(i + 1, len(a)):
                total = total + 2.0 * x * a[j] * weights[i + j]
        return total

    z, d, u, norm = [1.0], [1.0], [], m[0]
    for step in range(ITERS):
        alpha = norm / norm_of(d, gaps)
        u = [a + alpha * b for a, b in zip(u + [0.0], d)]
        shifted = [0.0] + d
        z = [a - alpha * (b - c) for a, b, c in zip(z + [0.0], d + [0.0], shifted)]
        if step < ITERS - 1:
            after = norm_of(z, m)
            ratio = after / norm
            d = [a + ratio * b for a, b in zip(z, d + [0.0])]
            norm = after
    return u, z


def gathered(copies, axis):
    return lax.all_to_all(copies, axis, 0, 0, tiled=True)


def kernel_call(body, *shapes, spaces, scratch=(), cost=None, room=32):
    out = [jax.ShapeDtypeStruct(shape, dtype) for shape, dtype in shapes]
    whole = pl.BlockSpec(memory_space=pltpu.VMEM)
    scalars = pl.BlockSpec(memory_space=pltpu.SMEM)
    return pl.pallas_call(
        body,
        out_shape=out,
        in_specs=[scalars if c == "s" else whole for c in spaces],
        out_specs=[whole] * len(out),
        scratch_shapes=scratch,
        cost_estimate=cost,
        compiler_params=pltpu.CompilerParams(vmem_limit_bytes=room * 2**20),
    )


def pack_kernel(weights, green, copies):
    count, size = green.shape[0], green.shape[1]
    half = size // 2
    row = lax.broadcasted_iota(jnp.int32, (half, half), 0)
    col = lax.broadcasted_iota(jnp.int32, (half, half), 1)

    def quarter(i, j):
        rows, cols = slice(i * half, (i + 1) * half), slice(j * half, (j + 1) * half)
        return sum(
            weights[:, e : e + 1] * green[e, rows, cols].astype(F32) for e in range(count)
        )

    low = quarter(1, 1)
    cross = quarter(0, 1).astype(BF16)
    mixed = jnp.where(row <= col, quarter(0, 0), low).astype(BF16)
    diagonal = jnp.sum(jnp.where(row == col, low, 0.0), axis=0, keepdims=True)
    tail = jnp.broadcast_to(diagonal, (16, half)).astype(BF16)
    for target in range(copies.shape[0]):
        copies[target, :half] = cross
        copies[target, half : 2 * half] = mixed
        copies[target, 2 * half :] = tail


def unpack_kernel(copies, density):
    half = density.shape[0] // 2

    def total(rows):
        parts = copies[0, rows].astype(F32)
        for i in range(1, copies.shape[0]):
            parts = parts + copies[i, rows].astype(F32)
        return parts.astype(BF16).astype(F32)

    row = lax.broadcasted_iota(jnp.int32, (half, half), 0)
    col = lax.broadcasted_iota(jnp.int32, (half, half), 1)
    cross = total(slice(0, half))
    mixed = total(slice(half, 2 * half))
    diagonal = total(slice(2 * half, 2 * half + 16))[:1]
    first = jnp.where(row < col, 2.0 * mixed, jnp.where(row == col, mixed, 0.0))
    last = jnp.where(row > col, 2.0 * mixed, jnp.where(row == col, diagonal, 0.0))
    density[:half, :half] = first.astype(BF16)
    density[:half, half:] = (2.0 * cross).astype(BF16)
    density[half:, :half] = jnp.zeros((half, half), BF16)
    density[half:, half:] = last.astype(BF16)


def in_three(value):
    pieces = []
    for _ in range(3):
        piece = lax.reduce_precision(value, 8, 7)
        pieces.append(piece.astype(BF16))
        value = value - piece
    return pieces


def edges_kernel(
    place, base, pot, charge, pair, pair_charge, outer, outer_charge, up, down, block
):
    layers, rows, depth = pot.shape
    even = jnp.broadcast_to(place[0:1], (HALO, depth)) > 0.5
    number = place[1:2]
    wide = rows + 8
    line = lax.broadcasted_iota(jnp.int32, (wide, depth), 0)
    gap = jnp.zeros((wide - rows - 2 * HALO, depth), F32)

    def joined(own, inner, far):
        above = jnp.where(even, inner, far)
        below = jnp.where(even, far, inner)
        return jnp.concatenate([own, above, gap, below], axis=0)

    ahead_here = (line == rows) | (line == 0)
    behind_here = (line == rows - 1) | (line == wide - 1)
    for x in range(layers):
        potential = joined(pot[x], pair[layers + x], outer[layers + x])
        value = joined(base[x], pair[x], outer[x])
        value = value + jnp.where(ahead_here, pltpu.roll(potential, 1, 0), 0.0)
        value = value + jnp.where(behind_here, pltpu.roll(potential, wide - 1, 0), 0.0)
        if x > layers - 1 - HALO:
            up[x - (layers - HALO)] = value
        if x < HALO:
            down[x] = value
        if x == layers - 1:
            up[HALO] = potential
        if x == 0:
            down[HALO] = potential
    own = joined(charge[...], pair_charge[...], outer_charge[...])
    own = jnp.where(line == rows + HALO, number, own)
    up[HALO + 1] = own
    down[HALO + 1] = own
    block[...] = own


def arrived_kernel(place, up, lowest, low, charge):
    rows = up.shape[1] - 8
    first = place[2:3]
    blocks = [lowest[...], low[HALO + 1], up[HALO + 1]]
    ids = [b[rows + HALO : rows + HALO + 1] for b in blocks]
    for x in range(charge.shape[0]):
        layer = first + float(x - HALO)
        total = jnp.zeros(lowest.shape, F32)
        for b, i in zip(blocks, ids):
            total = total + jnp.where(i == layer, b, 0.0)
        charge[x] = total


def powers_kernel(place, up, down, part, low, high, pot, w, mass_out, n2_out, handed, mine, copies):
    layers, rows, depth = pot.shape
    number, first = place[1:2], place[2:3]
    after_all = float(layers * copies.shape[0])
    wide = up.shape[1]
    edge = (wide - rows) // 2
    line = lax.broadcasted_iota(jnp.int32, (wide, depth), 0)
    cell = lax.broadcasted_iota(jnp.int32, (wide, depth), 1)
    not_first, not_last = cell > 0, cell < depth - 1
    inside = line < rows
    inside = inside | ((line < rows + edge) & (place[3:4] > 0.5))
    inside = inside | ((line >= rows + edge) & (place[4:5] > 0.5))

    def neighbours(v, x):
        centre = v[x]
        total = pltpu.roll(centre, 1, 0) + pltpu.roll(centre, wide - 1, 0)
        total = total + jnp.where(not_first, pltpu.roll(centre, 1, 1), 0.0)
        total = total + jnp.where(not_last, pltpu.roll(centre, depth - 1, 1), 0.0)
        return total + v[x - 1] + v[x + 1]

    last = high[HALO + 1]
    low_id, last_id = (b[HALO + 1, rows + HALO : rows + HALO + 1] for b in (low, high))
    w0, inverse, mass = {}, {}, {}
    for x in range(-HALO, layers + HALO):
        layer = first + float(x)
        if x < 0:
            value = low[x + HALO]
        elif x < HALO:
            value = down[x]
        elif x < layers:
            value = up[x - (layers - HALO)]
        else:
            value = high[x - layers]
        if x == -1:
            value = value + down[HALO]
        if x == 0:
            value = value + low[HALO]
        if x == layers - 1:
            value = value + high[HALO]
        if x == layers:
            value = value + up[HALO]
        charge = part[x + HALO] + jnp.where(last_id == layer, last, 0.0)
        mass[x] = 6.0 + charge * 0.25
        valid = inside & (layer > -0.5) & (layer < after_all - 0.5)
        inverse[x] = jnp.where(valid, 1.0 / mass[x], 0.0)
        w0[x] = inverse[x] * (value - charge)
    w1 = {x: inverse[x] * neighbours(w0, x) for x in range(1 - HALO, layers + HALO - 1)}
    w2 = {x: inverse[x] * neighbours(w1, x) for x in range(2 - HALO, layers + HALO - 2)}
    sums = [jnp.zeros((rows, depth), F32)] * 6
    on_mine = [jnp.zeros((rows, depth), F32)] * 4
    on_handed = [jnp.zeros((rows, depth), F32)] * 4
    for x in range(layers):
        m, a, b, c = (v[x][:rows] for v in (mass, w0, w1, w2))
        n2 = neighbours(w2, x)[:rows]
        mb, mc = m * b, m * c
        terms = (m * a * a, a * mb, b * mb, b * mc, c * mc, c * n2)
        sums = [t + u for t, u in zip(sums, terms)]
        w[0, x], w[1, x], w[2, x] = a, b, c
        mass_out[x] = m
        n2_out[x] = n2
        layer = first + float(x)
        fields = (a, b, c, pot[x])
        on_mine = [t + jnp.where(number == layer, u, 0.0) for t, u in zip(on_mine, fields)]
        theirs = low_id == layer
        on_handed = [t + jnp.where(theirs, u, 0.0) for t, u in zip(on_handed, fields)]
    for k in range(4):
        mine[k] = on_mine[k]
        handed[k] = on_handed[k]
    lane = lax.broadcasted_iota(jnp.int32, (1, copies.shape[1]), 1)
    row = jnp.zeros(lane.shape, F32)
    for k in range(6):
        row = row + jnp.where(lane == k, jnp.sum(sums[k], keepdims=True), 0.0)
    copies[...] = jnp.broadcast_to(row, copies.shape)


def onsite_kernel(basis, mine, theirs, out, sums):
    _, size, rows, depth = basis.shape
    chunk = 64
    field = (mine[...] + theirs[...]).reshape(4 * rows, depth)
    pieces = []
    for _ in range(3):
        piece = field.astype(BF16)
        pieces.append(piece)
        field = field - piece.astype(F32)
    pieces.append(jnp.zeros_like(piece))
    values = jnp.concatenate(pieces, axis=0)
    lanes = values.shape[0]
    contract = (((1,), (1,)), ((), ()))
    here = lax.broadcasted_iota(jnp.int32, (rows, lanes), 0)
    there = lax.broadcasted_iota(jnp.int32, (rows, lanes), 1)
    same = (there % rows == here).astype(F32)
    for start in range(0, size, chunk):
        part = basis[0, start : start + chunk].astype(F32)
        squared = (part * part).reshape(chunk * rows, depth)
        high = squared.astype(BF16)
        low = (squared - high.astype(F32)).astype(BF16)
        product = lax.dot_general(high, values, contract, preferred_element_type=F32)
        product = product + lax.dot_general(low, values, contract, preferred_element_type=F32)
        product = product.reshape(chunk, rows, lanes) * same[None]
        sums[start : start + chunk] = jnp.sum(product, axis=1)
    out_row = lax.broadcasted_iota(jnp.int32, (8, lanes), 0)
    out_lane = lax.broadcasted_iota(jnp.int32, (8, lanes), 1)
    pick = (out_lane % (4 * rows)) // rows == out_row
    pick = (pick & (out_lane < 12 * rows)).astype(F32)
    result = lax.dot_general(
        pick, sums[...], contract, precision=lax.Precision.HIGHEST, preferred_element_type=F32
    )
    out[...] = result


def finish_kernel(parts, w, mass, n2, pot, potential, residual, onsite):
    total = parts[0]
    for i in range(1, parts.shape[0]):
        total = total + parts[i]
    u, z = coefficients([total[4:5, i : i + 1] for i in range(6)])
    for x in range(pot.shape[0]):
        a, b, c = w[0, x], w[1, x], w[2, x]
        potential[x] = pot[x] + (u[0] * a + u[1] * b + u[2] * c)
        residual[x] = mass[x] * (z[0] * a + z[1] * b + z[2] * c) + z[3] * n2[x]
    onsite[...] = u[0] * total[0:1] + u[1] * total[1:2] + u[2] * total[2:3] + total[3:4]


def shards(green, weights, basis, block_layer, pot, dop):
    layers, rows, depth = pot.shape
    e, s = lax.axis_index("energy"), lax.axis_index("space")
    ne, ns = lax.axis_size("energy"), lax.axis_size("space")
    functions = basis[0]
    size = functions.shape[0]
    energies = green.shape[0]
    wide = rows + 8
    block = (layers, rows, depth)
    facts = [e % 2 == 0, block_layer[0], s * layers, e < ne - 1, e > 0, 0, 0, 0]
    place = jnp.broadcast_to(jnp.stack([jnp.asarray(f, F32) for f in facts])[:, None], (8, depth))

    packed_shape = (ne, size + 16, size // 2)
    (copies,) = kernel_call(pack_kernel, (packed_shape, BF16), spaces="vv", room=60)(
        weights[None], green.reshape(energies, size, size)
    )
    even = e % 2 == 0
    pairs = [(i, i ^ 1) for i in range(ne)]
    across = [(i, i + 1) for i in range(1, ne - 1, 2)]
    across = across + [(target, source) for source, target in across]

    late_basis, late_pot, late_dop, copies = lax.optimization_barrier((basis, pot, dop, copies))
    base = late_dop - 6.0 * late_pot + neighbours_in_block(late_pot)
    fields = jnp.concatenate([base, late_pot], axis=0)
    lines = jnp.concatenate([late_basis[0], *in_three(fields)], axis=0)
    lines = jnp.transpose(lines, (1, 0, 2))
    front, back = lines[:HALO], lines[-HALO:]
    pair = lax.ppermute(jnp.where(even, back, front), "energy", pairs)
    outer = lax.ppermute(jnp.where(even, front, back), "energy", across)

    (density,) = kernel_call(
        unpack_kernel,
        ((size, size), BF16),
        spaces="v",
        cost=pl.CostEstimate(flops=10**10, bytes_accessed=10**6, transcendentals=0),
    )(gathered(copies, "energy"))
    pair, pair_density = lax.optimization_barrier((pair, density))
    applied = jnp.einsum("ij,jyz->iyz", density, functions, preferred_element_type=F32)
    charge_block = jnp.sum(functions * applied, axis=0)

    def from_lines(received, density):
        values = received[:, :size]
        applied = jnp.einsum("ij,yjz->yiz", density, values, preferred_element_type=F32)
        pieces = jnp.split(received[:, size:].astype(F32), 3, axis=1)
        around = jnp.transpose(pieces[0] + pieces[1] + pieces[2], (1, 0, 2))
        return around, jnp.sum(values * applied, axis=1)

    pair_fields, pair_charge = from_lines(pair, pair_density)
    outer, outer_density, charge_block, pair_charge = lax.optimization_barrier(
        (outer, density, charge_block, pair_charge)
    )
    outer_fields, outer_charge = from_lines(outer, outer_density)
    message = ((HALO + 2, wide, depth), F32)
    up, down, own = kernel_call(
        edges_kernel, message, message, ((wide, depth), F32), spaces="vvvvvvvv"
    )(
        place,
        base,
        pot,
        charge_block,
        pair_fields,
        pair_charge,
        outer_fields,
        outer_charge,
    )
    lowest = moved(own, "space", 2)
    low = moved(up, "space", 1)
    high = moved(down, "space", -1)

    (part,) = kernel_call(
        arrived_kernel,
        ((layers + 2 * HALO, wide, depth), F32),
        spaces="vvvv",
        cost=pl.CostEstimate(flops=8 * 10**9, bytes_accessed=10**6, transcendentals=0),
    )(place, up, lowest, low)
    field, four = (block, F32), ((4, rows, depth), F32)
    w, mass, n2, handed, mine, copies = kernel_call(
        powers_kernel,
        ((3,) + block, F32),
        field,
        field,
        four,
        four,
        ((ns, 128), F32),
        spaces="vvvvvvv",
    )(place, up, down, part, low, high, pot)
    row = jnp.sum(gathered(copies, "space"), axis=0)
    theirs = moved(handed, "space", -1)
    (parts,) = kernel_call(
        onsite_kernel,
        ((8, size), F32),
        spaces="vvv",
        scratch=[pltpu.VMEM((size, 16 * rows), F32)],
        cost=pl.CostEstimate(
            flops=2 * 256 * size * rows * depth, bytes_accessed=2 * size * rows * depth, transcendentals=0
        ),
    )(basis, mine, theirs)
    row = jnp.pad(row[None], ((4, 3), (0, size - 128)))
    parts = parts + row
    parts = gathered(jnp.broadcast_to(parts[None], (ne,) + parts.shape), "energy")
    potential, residual, onsite = kernel_call(
        finish_kernel, field, field, ((1, size), F32), spaces="vvvvv"
    )(parts, w, mass, n2, pot)
    return (potential, residual, onsite)


def solution(mesh):
    in_specs = (
        P("energy", "space", None, None),
        P("energy"),
        P("space", None, "energy", None),
        P("space"),
        P("space", "energy", None),
        P("space", "energy", None),
    )
    out_specs = (P("space", "energy", None), P("space", "energy", None), P("space", None))
    return jax.shard_map(shards, mesh=mesh, in_specs=in_specs, out_specs=out_specs, check_vma=False)
```

profile of v0, /device:TPU:1, one launch (start us, length us, event | category | flops | bytes accessed | tf_op | source)
XLA Modules:
  0.0 75.7 jit_solution(14078330497487406156)
XLA Ops:
  0.6 0.0 copy-start.1
  0.6 0.0 copy-start.2
  0.7 0.0 copy-start
  0.7 2.0 %shard_map.85 = bf16[8,272,128]{2,1,0:T(8,128)(2,1)} custom-call(f32[1,2]{1,0:T(1,128)} %bitcast.42, bf16[2,256,256]{2,1,0:T(8,128)(2,1)} %bitcast.40), custom_call_target="tpu_custom_call" | custom-call | tf_op jit(solution)/shard_map/pallas_call | solution.py:322
  2.7 10.3 %all-to-all-start = ((bf16[8,272,128]{2,1,0:T(8,128)(2,1)}), bf16[8,272,128]{2,1,0:T(8,128)(2,1)S(1)}, u32[]{:S(2)}, u32[]{:S(2)}) async-start(bf16[8,272,128]{2,1,0:T(8,128)(2,1)} %shard_map.85), calls=%async_computation | async-start | bytes 1114112 | tf_op jit(solution)/shard_map/all_to_all | solution.py:65
  13.0 0.0 copy-done.1
  13.0 0.1 fusion.20
  13.1 0.0 copy-done.2
  13.1 0.1 fusion.17.base
  13.2 0.0 copy-done
  13.3 0.2 copy.27
  13.5 0.1 maximum_bitcast_fusion
  13.6 0.1 broadcast_select_fusion
  13.6 2.0 %collective-permute-start.1 = (bf16[3,280,256]{2,1,0:T(8,128)(2,1)S(1)}, bf16[3,280,256]{2,1,0:T(8,128)(2,1)S(1)}, u32[]{:S(2)}, u32[]{:S(2)}) collective-permute-start(bf16[3,280,256]{2,1,0:T(8,128)(2,1)S(1)} %get-tuple-element.41), channel_id=1, source_target_pairs={{0,64},{64,0},{128,192},{192,128},{256,320},{320,256},{384,448},{4... | collective-permute-start | bytes 1290248 | tf_op jit(solution)/shard_map/ppermute | solution.py:336
  15.7 3.6 %collective-permute-start = (bf16[3,280,256]{2,1,0:T(8,128)(2,1)S(1)}, bf16[3,280,256]{2,1,0:T(8,128)(2,1)S(1)}, u32[]{:S(2)}, u32[]{:S(2)}) collective-permute-start(bf16[3,280,256]{2,1,0:T(8,128)(2,1)S(1)} %get-tuple-element.42), channel_id=1, source_target_pairs={{64,128},{192,256},{320,384},{128,64},{256,192},{384,320},{65,129}... | collective-permute-start | bytes 1290248 | tf_op jit(solution)/shard_map/ppermute | solution.py:337
  19.9 0.1 stack.32
  20.0 2.8 %all-to-all-done.copies = bf16[8,272,128]{2,1,0:T(8,128)(2,1)S(1)} async-done(((bf16[8,272,128]{2,1,0:T(8,128)(2,1)}), bf16[8,272,128]{2,1,0:T(8,128)(2,1)S(1)}, u32[]{:S(2)}, u32[]{:S(2)}) %all-to-all-start) | async-done | bytes 557088 | tf_op jit(solution)/shard_map/all_to_all | solution.py:65
  22.8 0.1 shard_map.86
  23.0 0.0 collective-permute-done.1
  23.0 0.2 copy.19
  23.2 0.3 multiply_reduce_fusion.2.pair_charge
  23.5 0.5 multiply_reduce_fusion.charge
  24.0 2.1 %collective-permute-done = bf16[3,280,256]{2,1,0:T(8,128)(2,1)S(1)} collective-permute-done((bf16[3,280,256]{2,1,0:T(8,128)(2,1)S(1)}, bf16[3,280,256]{2,1,0:T(8,128)(2,1)S(1)}, u32[]{:S(2)}, u32[]{:S(2)}) %collective-permute-start) | collective-permute-done | bytes 430112 | tf_op jit(solution)/shard_map/ppermute | solution.py:337
  26.1 0.2 copy.20
  26.3 0.3 multiply_reduce_fusion.1.outer_charge
  26.7 0.1 broadcast_in_dim.8.place
  26.8 1.3 %collective-permute-start.3 = (f32[5,16,256]{2,1,0:T(8,128)S(1)}, f32[5,16,256]{2,1,0:T(8,128)S(1)}, u32[]{:S(2)}, u32[]{:S(2)}) collective-permute-start(f32[5,16,256]{2,1,0:T(8,128)S(1)} %get-tuple-element.32.up), channel_id=1, source_target_pairs={{0,1},{1,2},{2,3},{3,4},{4,5},{5,6},{6,7},{7,8},{8,9},{9,10},{10,1... | collective-permute-start | bytes 245768 | tf_op jit(solution)/shard_map/ppermute | solution.py:17
  28.1 4.0 %collective-permute-start.2 = (f32[16,256]{1,0:T(8,128)S(1)}, f32[16,256]{1,0:T(8,128)S(1)}, u32[]{:S(2)}, u32[]{:S(2)}) collective-permute-start(f32[16,256]{1,0:T(8,128)S(1)} %get-tuple-element.34), channel_id=1, source_target_pairs={{0,2},{1,3},{2,4},{3,5},{4,6},{5,7},{6,8},{7,9},{8,10},{9,11},{10,... | collective-permute-start | bytes 49160 | tf_op jit(solution)/shard_map/ppermute | solution.py:17
  32.1 1.3 %collective-permute-start.4 = (f32[5,16,256]{2,1,0:T(8,128)S(1)}, f32[5,16,256]{2,1,0:T(8,128)S(1)}, u32[]{:S(2)}, u32[]{:S(2)}) collective-permute-start(f32[5,16,256]{2,1,0:T(8,128)S(1)} %get-tuple-element.33.down), channel_id=1, source_target_pairs={{1,0},{2,1},{3,2},{4,3},{5,4},{6,5},{7,6},{8,7},{9,8},{10,9},{11,1... | collective-permute-start | bytes 245768 | tf_op jit(solution)/shard_map/ppermute | solution.py:17
  33.4 0.0 collective-permute-done.2.lowest
  33.4 0.0 collective-permute-done.3.low
  33.4 0.1 shard_map.88.part
  33.5 6.6 %collective-permute-done.4.high = f32[5,16,256]{2,1,0:T(8,128)S(1)} collective-permute-done((f32[5,16,256]{2,1,0:T(8,128)S(1)}, f32[5,16,256]{2,1,0:T(8,128)S(1)}, u32[]{:S(2)}, u32[]{:S(2)}) %collective-permute-start.4) | collective-permute-done | bytes 81952 | tf_op jit(solution)/shard_map/ppermute | solution.py:17
  40.1 1.0 %shard_map.89 = (f32[3,4,8,256]{3,2,1,0:T(8,128)S(1)}, f32[4,8,256]{2,1,0:T(8,128)S(1)}, f32[4,8,256]{2,1,0:T(8,128)S(1)}, f32[4,8,256]{2,1,0:T(8,128)S(1)}, f32...) custom-call(f32[8,256]{1,0:T(8,128)S(1)} %broadcast_in_dim.8.place, f32[5,16,256]{2,1,0:T(8,128)S(1)} %get-tuple-element.32.up, ...), custom_call_target="tpu_custom_call" | custom-call | tf_op jit(solution)/shard_map/pallas_call | solution.py:385
  41.1 12.1 %all-to-all-start.1 = ((f32[64,1,128]{2,1,0:T(1,128)}), f32[64,1,128]{2,1,0:T(1,128)S(1)}, u32[]{:S(2)}, u32[]{:S(2)}) async-start(f32[64,1,128]{2,1,0:T(1,128)} %bitcast.17), calls=%async_computation.1 | async-start | bytes 65536 | tf_op jit(solution)/shard_map/all_to_all | solution.py:65
  53.2 1.3 %collective-permute-start.5 = (f32[4,8,256]{2,1,0:T(8,128)S(1)}, f32[4,8,256]{2,1,0:T(8,128)S(1)}, u32[]{:S(2)}, u32[]{:S(2)}) collective-permute-start(f32[4,8,256]{2,1,0:T(8,128)S(1)} %get-tuple-element.36), channel_id=1, source_target_pairs={{1,0},{2,1},{3,2},{4,3},{5,4},{6,5},{7,6},{8,7},{9,8},{10,9},{11,1... | collective-permute-start | bytes 98312 | tf_op jit(solution)/shard_map/ppermute | solution.py:17
  54.5 3.7 %collective-permute-done.5.theirs = f32[4,8,256]{2,1,0:T(8,128)S(1)} collective-permute-done((f32[4,8,256]{2,1,0:T(8,128)S(1)}, f32[4,8,256]{2,1,0:T(8,128)S(1)}, u32[]{:S(2)}, u32[]{:S(2)}) %collective-permute-start.5) | collective-permute-done | bytes 32800 | tf_op jit(solution)/shard_map/ppermute | solution.py:17
  58.2 1.1 %shard_map.90 = f32[8,256]{1,0:T(8,128)S(1)} custom-call(bf16[1,256,8,256]{3,2,1,0:T(8,128)(2,1)S(1)} %copy-done, f32[4,8,256]{2,1,0:T(8,128)S(1)} %get-tuple-element.35.mine, f32[4,8,256]{2,1,0:T(8,128)S(1)} %collective-permute-done.5.theirs), custom_call_target="tpu_custom_call" | custom-call | flops 268435456 | bytes 1048576 | tf_op jit(solution)/shard_map/pallas_call | solution.py:397
  59.3 4.7 %all-to-all-done.1 = f32[64,1,128]{2,1,0:T(1,128)S(1)} async-done(((f32[64,1,128]{2,1,0:T(1,128)}), f32[64,1,128]{2,1,0:T(1,128)S(1)}, u32[]{:S(2)}, u32[]{:S(2)}) %all-to-all-start.1) | async-done | bytes 32800 | tf_op jit(solution)/shard_map/all_to_all | solution.py:65
  64.0 0.1 reduce_sum.39
  64.1 10.8 %all_to_all.19.parts = f32[8,8,256]{2,1,0:T(8,128)S(1)} all-to-all(f32[8,8,256]{2,1,0:T(8,128)S(1)} %broadcast_in_dim.22), channel_id=1, replica_groups=mesh['energy'=8,'space'=64] {'energy'}, dimensions={0} | all-to-all | bytes 131072 | tf_op jit(solution)/shard_map/all_to_all | solution.py:65
  74.9 0.9 %shard_map.91 = (f32[4,8,256]{2,1,0:T(8,128)}, f32[4,8,256]{2,1,0:T(8,128)}, f32[1,256]{1,0:T(1,128)}) custom-call(f32[8,8,256]{2,1,0:T(8,128)S(1)} %all_to_all.19.parts, f32[3,4,8,256]{3,2,1,0:T(8,128)S(1)} %get-tuple-element.38.w, f32[4,8,256]{2,1,0:T(8,128)S(1)} %get-tuple-element.39.mass, f32[4,8,256]{2,1,0:T(8,128)S(1)} %get-tuple-element.40.n2, ...), custom_call_target="tpu_custom_call" | custom-call | tf_op jit(solution)/shard_map/pallas_call | solution.py:409
  (11 shorter events, 0.2 us)
Async XLA Ops:
  0.6 12.4 %copy-start.1 = (f32[4,8,256]{2,1,0:T(8,128)S(1)}, f32[4,8,256]{2,1,0:T(8,128)}, u32[]{:S(2)}) copy-start(f32[4,8,256]{2,1,0:T(8,128)} %pot.5) | copy-start | bytes 98308
  0.6 12.4 %copy-start.2 = (f32[4,8,256]{2,1,0:T(8,128)S(1)}, f32[4,8,256]{2,1,0:T(8,128)}, u32[]{:S(2)}) copy-start(f32[4,8,256]{2,1,0:T(8,128)} %param.11) | copy-start | bytes 98308
  0.7 12.6 %copy-start = (bf16[1,256,8,256]{3,2,1,0:T(8,128)(2,1)S(1)}, bf16[1,256,8,256]{3,2,1,0:T(8,128)(2,1)}, u32[]{:S(2)}) copy-start(bf16[1,256,8,256]{3,2,1,0:T(8,128)(2,1)} %basis.1) | copy-start | bytes 3145732
  2.7 20.2 %all-to-all-start = ((bf16[8,272,128]{2,1,0:T(8,128)(2,1)}), bf16[8,272,128]{2,1,0:T(8,128)(2,1)S(1)}, u32[]{:S(2)}, u32[]{:S(2)}) async-start(bf16[8,272,128]{2,1,0:T(8,128)(2,1)} %shard_map.85), calls=%async_computation | async-start | bytes 1114112 | tf_op jit(solution)/shard_map/all_to_all | solution.py:65
  13.6 9.3 %collective-permute-start.1 = (bf16[3,280,256]{2,1,0:T(8,128)(2,1)S(1)}, bf16[3,280,256]{2,1,0:T(8,128)(2,1)S(1)}, u32[]{:S(2)}, u32[]{:S(2)}) collective-permute-start(bf16[3,280,256]{2,1,0:T(8,128)(2,1)S(1)} %get-tuple-element.41), channel_id=1, source_target_pairs={{0,64},{64,0},{128,192},{192,128},{256,320},{320,256},{384,448},{4... | collective-permute-start | bytes 1290248 | tf_op jit(solution)/shard_map/ppermute | solution.py:336
  15.7 10.4 %collective-permute-start = (bf16[3,280,256]{2,1,0:T(8,128)(2,1)S(1)}, bf16[3,280,256]{2,1,0:T(8,128)(2,1)S(1)}, u32[]{:S(2)}, u32[]{:S(2)}) collective-permute-start(bf16[3,280,256]{2,1,0:T(8,128)(2,1)S(1)} %get-tuple-element.42), channel_id=1, source_target_pairs={{64,128},{192,256},{320,384},{128,64},{256,192},{384,320},{65,129}... | collective-permute-start | bytes 1290248 | tf_op jit(solution)/shard_map/ppermute | solution.py:337
  26.8 6.6 %collective-permute-start.3 = (f32[5,16,256]{2,1,0:T(8,128)S(1)}, f32[5,16,256]{2,1,0:T(8,128)S(1)}, u32[]{:S(2)}, u32[]{:S(2)}) collective-permute-start(f32[5,16,256]{2,1,0:T(8,128)S(1)} %get-tuple-element.32.up), channel_id=1, source_target_pairs={{0,1},{1,2},{2,3},{3,4},{4,5},{5,6},{6,7},{7,8},{8,9},{9,10},{10,1... | collective-permute-start | bytes 245768 | tf_op jit(solution)/shard_map/ppermute | solution.py:17
  28.1 5.3 %collective-permute-start.2 = (f32[16,256]{1,0:T(8,128)S(1)}, f32[16,256]{1,0:T(8,128)S(1)}, u32[]{:S(2)}, u32[]{:S(2)}) collective-permute-start(f32[16,256]{1,0:T(8,128)S(1)} %get-tuple-element.34), channel_id=1, source_target_pairs={{0,2},{1,3},{2,4},{3,5},{4,6},{5,7},{6,8},{7,9},{8,10},{9,11},{10,... | collective-permute-start | bytes 49160 | tf_op jit(solution)/shard_map/ppermute | solution.py:17
  32.1 8.0 %collective-permute-start.4 = (f32[5,16,256]{2,1,0:T(8,128)S(1)}, f32[5,16,256]{2,1,0:T(8,128)S(1)}, u32[]{:S(2)}, u32[]{:S(2)}) collective-permute-start(f32[5,16,256]{2,1,0:T(8,128)S(1)} %get-tuple-element.33.down), channel_id=1, source_target_pairs={{1,0},{2,1},{3,2},{4,3},{5,4},{6,5},{7,6},{8,7},{9,8},{10,9},{11,1... | collective-permute-start | bytes 245768 | tf_op jit(solution)/shard_map/ppermute | solution.py:17
  41.1 22.9 %all-to-all-start.1 = ((f32[64,1,128]{2,1,0:T(1,128)}), f32[64,1,128]{2,1,0:T(1,128)S(1)}, u32[]{:S(2)}, u32[]{:S(2)}) async-start(f32[64,1,128]{2,1,0:T(1,128)} %bitcast.17), calls=%async_computation.1 | async-start | bytes 65536 | tf_op jit(solution)/shard_map/all_to_all | solution.py:65
  53.2 5.0 %collective-permute-start.5 = (f32[4,8,256]{2,1,0:T(8,128)S(1)}, f32[4,8,256]{2,1,0:T(8,128)S(1)}, u32[]{:S(2)}, u32[]{:S(2)}) collective-permute-start(f32[4,8,256]{2,1,0:T(8,128)S(1)} %get-tuple-element.36), channel_id=1, source_target_pairs={{1,0},{2,1},{3,2},{4,3},{5,4},{6,5},{7,6},{8,7},{9,8},{10,9},{11,1... | collective-permute-start | bytes 98312 | tf_op jit(solution)/shard_map/ppermute | solution.py:17
where the time goes:
time: 76.2 us; the launch traced here: 75.7 us
  starting transfers between devices  35.9 us (47%)
  waiting for transfers between devices  19.9 us (26%)
  blocking collectives  10.8 us (14%)
  Pallas kernels  5.17 us (7%)
  between operations  1.55 us (2%)
  matrix products  1.06 us (1%)
  local copies, waits for them, and re-layouts  0.94 us (1%)
    all_to_all x2, starting transfers between devices, gathered(): return lax.all_to_all(copies, axis, 0, 0, tiled=True)  22.4 us
    all_to_all x1, blocking collectives, gathered(): return lax.all_to_all(copies, axis, 0, 0, tiled=True)  10.8 us
    ppermute x4, waiting for transfers between devices, moved(): return lax.ppermute(value, axis, pairs)  10.3 us
    ppermute x4, starting transfers between devices, moved(): return lax.ppermute(value, axis, pairs)  7.87 us
    all_to_all x2, waiting for transfers between devices, gathered(): return lax.all_to_all(copies, axis, 0, 0, tiled=True)  7.54 us
    ppermute x1, starting transfers between devices, shards(): outer = lax.ppermute(jnp.where(even, front, back), 'energy', across)  3.57 us
    ppermute x1, waiting for transfers between devices, shards(): outer = lax.ppermute(jnp.where(even, front, back), 'energy', across)  2.12 us
    ppermute x1, starting transfers between devices, shards(): pair = lax.ppermute(jnp.where(even, back, front), 'energy', pairs)  2.04 us
  transfers between devices with their start and end apart: 8, of which 5 were waited for; matrix products, arithmetic and copies ran while one was open for 2% of the time, Pallas kernels for 2%

commit v1 on v0

--- a/solution.py
+++ b/solution.py
@@ -342,7 +342,6 @@
         spaces="v",
         cost=pl.CostEstimate(flops=10**10, bytes_accessed=10**6, transcendentals=0),
     )(gathered(copies, "energy"))
-    pair, pair_density = lax.optimization_barrier((pair, density))
     applied = jnp.einsum("ij,jyz->iyz", density, functions, preferred_element_type=F32)
     charge_block = jnp.sum(functions * applied, axis=0)
 
@@ -353,11 +352,10 @@
         around = jnp.transpose(pieces[0] + pieces[1] + pieces[2], (1, 0, 2))
         return around, jnp.sum(values * applied, axis=1)
 
+    outer, outer_density, charge_block = lax.optimization_barrier((outer, density, charge_block))
+    outer_fields, outer_charge = from_lines(outer, outer_density)
+    pair, pair_density, outer_charge = lax.optimization_barrier((pair, density, outer_charge))
     pair_fields, pair_charge = from_lines(pair, pair_density)
-    outer, outer_density, charge_block, pair_charge = lax.optimization_barrier(
-        (outer, density, charge_block, pair_charge)
-    )
-    outer_fields, outer_charge = from_lines(outer, outer_density)
     message = ((HALO + 2, wide, depth), F32)
     up, down, own = kernel_call(
         edges_kernel, message, message, ((wide, depth), F32), spaces="vvvvvvvv"

time: 76.2 us -> 76.7 us (level)
  no operation moved by 1% of the time
where the time goes in v1:
time: 76.7 us; the launch traced here: 76.3 us
  starting transfers between devices  36.1 us (47%)
  waiting for transfers between devices  19.8 us (26%)
  blocking collectives  11.3 us (15%)
  Pallas kernels  5.17 us (7%)
  between operations  1.55 us (2%)
  matrix products  1.05 us (1%)
  local copies, waits for them, and re-layouts  0.94 us (1%)
    all_to_all x2, starting transfers between devices, gathered(): return lax.all_to_all(copies, axis, 0, 0, tiled=True)  22.6 us
    all_to_all x1, blocking collectives, gathered(): return lax.all_to_all(copies, axis, 0, 0, tiled=True)  11.3 us
    ppermute x4, waiting for transfers between devices, moved(): return lax.ppermute(value, axis, pairs)  9.54 us
    ppermute x4, starting transfers between devices, moved(): return lax.ppermute(value, axis, pairs)  7.87 us
    all_to_all x2, waiting for transfers between devices, gathered(): return lax.all_to_all(copies, axis, 0, 0, tiled=True)  7.54 us
    ppermute x1, starting transfers between devices, shards(): outer = lax.ppermute(jnp.where(even, front, back), 'energy', across)  3.57 us
    ppermute x1, waiting for transfers between devices, shards(): outer = lax.ppermute(jnp.where(even, front, back), 'energy', across)  2.67 us
    ppermute x1, starting transfers between devices, shards(): pair = lax.ppermute(jnp.where(even, back, front), 'energy', pairs)  2.04 us
  transfers between devices with their start and end apart: 8, of which 5 were waited for; matrix products, arithmetic and copies ran while one was open for 2% of the time, Pallas kernels for 2%

profile of v1, /device:TPU:1, one launch (start us, length us, event | category | flops | bytes accessed | tf_op | source)
XLA Modules:
  0.0 76.3 jit_solution(4400151028627960305)
XLA Ops:
  0.6 0.0 copy-start.1
  0.6 0.0 copy-start.2
  0.7 0.0 copy-start
  0.7 2.0 %shard_map.85 = bf16[8,272,128]{2,1,0:T(8,128)(2,1)} custom-call(f32[1,2]{1,0:T(1,128)} %bitcast.42, bf16[2,256,256]{2,1,0:T(8,128)(2,1)} %bitcast.40), custom_call_target="tpu_custom_call" | custom-call | tf_op jit(solution)/shard_map/pallas_call | solution.py:322
  2.7 10.3 %all-to-all-start = ((bf16[8,272,128]{2,1,0:T(8,128)(2,1)}), bf16[8,272,128]{2,1,0:T(8,128)(2,1)S(1)}, u32[]{:S(2)}, u32[]{:S(2)}) async-start(bf16[8,272,128]{2,1,0:T(8,128)(2,1)} %shard_map.85), calls=%async_computation | async-start | bytes 1114112 | tf_op jit(solution)/shard_map/all_to_all | solution.py:65
  13.0 0.0 copy-done.1
  13.0 0.1 fusion.20
  13.1 0.0 copy-done.2
  13.1 0.1 fusion.17.base
  13.2 0.0 copy-done
  13.3 0.2 copy.27
  13.5 0.1 maximum_bitcast_fusion
  13.6 0.1 broadcast_select_fusion
  13.6 2.0 %collective-permute-start.1 = (bf16[3,280,256]{2,1,0:T(8,128)(2,1)S(1)}, bf16[3,280,256]{2,1,0:T(8,128)(2,1)S(1)}, u32[]{:S(2)}, u32[]{:S(2)}) collective-permute-start(bf16[3,280,256]{2,1,0:T(8,128)(2,1)S(1)} %get-tuple-element.41), channel_id=1, source_target_pairs={{0,64},{64,0},{128,192},{192,128},{256,320},{320,256},{384,448},{4... | collective-permute-start | bytes 1290248 | tf_op jit(solution)/shard_map/ppermute | solution.py:336
  15.7 3.6 %collective-permute-start = (bf16[3,280,256]{2,1,0:T(8,128)(2,1)S(1)}, bf16[3,280,256]{2,1,0:T(8,128)(2,1)S(1)}, u32[]{:S(2)}, u32[]{:S(2)}) collective-permute-start(bf16[3,280,256]{2,1,0:T(8,128)(2,1)S(1)} %get-tuple-element.42), channel_id=1, source_target_pairs={{64,128},{192,256},{320,384},{128,64},{256,192},{384,320},{65,129}... | collective-permute-start | bytes 1290248 | tf_op jit(solution)/shard_map/ppermute | solution.py:337
  19.9 0.1 stack.32
  20.0 2.8 %all-to-all-done.copies = bf16[8,272,128]{2,1,0:T(8,128)(2,1)S(1)} async-done(((bf16[8,272,128]{2,1,0:T(8,128)(2,1)}), bf16[8,272,128]{2,1,0:T(8,128)(2,1)S(1)}, u32[]{:S(2)}, u32[]{:S(2)}) %all-to-all-start) | async-done | bytes 557088 | tf_op jit(solution)/shard_map/all_to_all | solution.py:65
  22.8 0.1 shard_map.86
  23.0 0.5 multiply_reduce_fusion.charge
  23.4 2.7 %collective-permute-done = bf16[3,280,256]{2,1,0:T(8,128)(2,1)S(1)} collective-permute-done((bf16[3,280,256]{2,1,0:T(8,128)(2,1)S(1)}, bf16[3,280,256]{2,1,0:T(8,128)(2,1)S(1)}, u32[]{:S(2)}, u32[]{:S(2)}) %collective-permute-start) | collective-permute-done | bytes 430112 | tf_op jit(solution)/shard_map/ppermute | solution.py:337
  26.1 0.2 copy.20
  26.3 0.3 multiply_reduce_fusion.2.outer_charge
  26.6 0.0 collective-permute-done.1
  26.6 0.2 copy.19
  26.9 0.3 multiply_reduce_fusion.1.pair_charge
  27.2 0.1 broadcast_in_dim.8.place
  27.3 1.3 %collective-permute-start.3 = (f32[5,16,256]{2,1,0:T(8,128)S(1)}, f32[5,16,256]{2,1,0:T(8,128)S(1)}, u32[]{:S(2)}, u32[]{:S(2)}) collective-permute-start(f32[5,16,256]{2,1,0:T(8,128)S(1)} %get-tuple-element.32.up), channel_id=1, source_target_pairs={{0,1},{1,2},{2,3},{3,4},{4,5},{5,6},{6,7},{7,8},{8,9},{9,10},{10,1... | collective-permute-start | bytes 245768 | tf_op jit(solution)/shard_map/ppermute | solution.py:17
  28.6 4.0 %collective-permute-start.2 = (f32[16,256]{1,0:T(8,128)S(1)}, f32[16,256]{1,0:T(8,128)S(1)}, u32[]{:S(2)}, u32[]{:S(2)}) collective-permute-start(f32[16,256]{1,0:T(8,128)S(1)} %get-tuple-element.34), channel_id=1, source_target_pairs={{0,2},{1,3},{2,4},{3,5},{4,6},{5,7},{6,8},{7,9},{8,10},{9,11},{10,... | collective-permute-start | bytes 49160 | tf_op jit(solution)/shard_map/ppermute | solution.py:17
  32.6 1.3 %collective-permute-start.4 = (f32[5,16,256]{2,1,0:T(8,128)S(1)}, f32[5,16,256]{2,1,0:T(8,128)S(1)}, u32[]{:S(2)}, u32[]{:S(2)}) collective-permute-start(f32[5,16,256]{2,1,0:T(8,128)S(1)} %get-tuple-element.33.down), channel_id=1, source_target_pairs={{1,0},{2,1},{3,2},{4,3},{5,4},{6,5},{7,6},{8,7},{9,8},{10,9},{11,1... | collective-permute-start | bytes 245768 | tf_op jit(solution)/shard_map/ppermute | solution.py:17
  33.9 0.0 collective-permute-done.2.lowest
  34.0 0.0 collective-permute-done.3.low
  34.0 0.1 shard_map.88.part
  34.0 5.8 %collective-permute-done.4.high = f32[5,16,256]{2,1,0:T(8,128)S(1)} collective-permute-done((f32[5,16,256]{2,1,0:T(8,128)S(1)}, f32[5,16,256]{2,1,0:T(8,128)S(1)}, u32[]{:S(2)}, u32[]{:S(2)}) %collective-permute-start.4) | collective-permute-done | bytes 81952 | tf_op jit(solution)/shard_map/ppermute | solution.py:17
  39.9 1.0 %shard_map.89 = (f32[3,4,8,256]{3,2,1,0:T(8,128)S(1)}, f32[4,8,256]{2,1,0:T(8,128)S(1)}, f32[4,8,256]{2,1,0:T(8,128)S(1)}, f32[4,8,256]{2,1,0:T(8,128)S(1)}, f32...) custom-call(f32[8,256]{1,0:T(8,128)S(1)} %broadcast_in_dim.8.place, f32[5,16,256]{2,1,0:T(8,128)S(1)} %get-tuple-element.32.up, ...), custom_call_target="tpu_custom_call" | custom-call | tf_op jit(solution)/shard_map/pallas_call | solution.py:383
  40.9 12.3 %all-to-all-start.1 = ((f32[64,1,128]{2,1,0:T(1,128)}), f32[64,1,128]{2,1,0:T(1,128)S(1)}, u32[]{:S(2)}, u32[]{:S(2)}) async-start(f32[64,1,128]{2,1,0:T(1,128)} %bitcast.17), calls=%async_computation.1 | async-start | bytes 65536 | tf_op jit(solution)/shard_map/all_to_all | solution.py:65
  53.2 1.3 %collective-permute-start.5 = (f32[4,8,256]{2,1,0:T(8,128)S(1)}, f32[4,8,256]{2,1,0:T(8,128)S(1)}, u32[]{:S(2)}, u32[]{:S(2)}) collective-permute-start(f32[4,8,256]{2,1,0:T(8,128)S(1)} %get-tuple-element.36), channel_id=1, source_target_pairs={{1,0},{2,1},{3,2},{4,3},{5,4},{6,5},{7,6},{8,7},{9,8},{10,9},{11,1... | collective-permute-start | bytes 98312 | tf_op jit(solution)/shard_map/ppermute | solution.py:17
  54.5 3.7 %collective-permute-done.5.theirs = f32[4,8,256]{2,1,0:T(8,128)S(1)} collective-permute-done((f32[4,8,256]{2,1,0:T(8,128)S(1)}, f32[4,8,256]{2,1,0:T(8,128)S(1)}, u32[]{:S(2)}, u32[]{:S(2)}) %collective-permute-start.5) | collective-permute-done | bytes 32800 | tf_op jit(solution)/shard_map/ppermute | solution.py:17
  58.2 1.1 %shard_map.90 = f32[8,256]{1,0:T(8,128)S(1)} custom-call(bf16[1,256,8,256]{3,2,1,0:T(8,128)(2,1)S(1)} %copy-done, f32[4,8,256]{2,1,0:T(8,128)S(1)} %get-tuple-element.35.mine, f32[4,8,256]{2,1,0:T(8,128)S(1)} %collective-permute-done.5.theirs), custom_call_target="tpu_custom_call" | custom-call | flops 268435456 | bytes 1048576 | tf_op jit(solution)/shard_map/pallas_call | solution.py:395
  59.3 4.7 %all-to-all-done.1 = f32[64,1,128]{2,1,0:T(1,128)S(1)} async-done(((f32[64,1,128]{2,1,0:T(1,128)}), f32[64,1,128]{2,1,0:T(1,128)S(1)}, u32[]{:S(2)}, u32[]{:S(2)}) %all-to-all-start.1) | async-done | bytes 32800 | tf_op jit(solution)/shard_map/all_to_all | solution.py:65
  64.0 0.1 reduce_sum.39
  64.1 11.3 %all_to_all.19.parts = f32[8,8,256]{2,1,0:T(8,128)S(1)} all-to-all(f32[8,8,256]{2,1,0:T(8,128)S(1)} %broadcast_in_dim.22), channel_id=1, replica_groups=mesh['energy'=8,'space'=64] {'energy'}, dimensions={0} | all-to-all | bytes 131072 | tf_op jit(solution)/shard_map/all_to_all | solution.py:65
  75.4 0.9 %shard_map.91 = (f32[4,8,256]{2,1,0:T(8,128)}, f32[4,8,256]{2,1,0:T(8,128)}, f32[1,256]{1,0:T(1,128)}) custom-call(f32[8,8,256]{2,1,0:T(8,128)S(1)} %all_to_all.19.parts, f32[3,4,8,256]{3,2,1,0:T(8,128)S(1)} %get-tuple-element.38.w, f32[4,8,256]{2,1,0:T(8,128)S(1)} %get-tuple-element.39.mass, f32[4,8,256]{2,1,0:T(8,128)S(1)} %get-tuple-element.40.n2, ...), custom_call_target="tpu_custom_call" | custom-call | tf_op jit(solution)/shard_map/pallas_call | solution.py:407
  (11 shorter events, 0.2 us)
Async XLA Ops:
  0.6 12.4 %copy-start.1 = (f32[4,8,256]{2,1,0:T(8,128)S(1)}, f32[4,8,256]{2,1,0:T(8,128)}, u32[]{:S(2)}) copy-start(f32[4,8,256]{2,1,0:T(8,128)} %pot.5) | copy-start | bytes 98308
  0.6 12.4 %copy-start.2 = (f32[4,8,256]{2,1,0:T(8,128)S(1)}, f32[4,8,256]{2,1,0:T(8,128)}, u32[]{:S(2)}) copy-start(f32[4,8,256]{2,1,0:T(8,128)} %param.11) | copy-start | bytes 98308
  0.7 12.6 %copy-start = (bf16[1,256,8,256]{3,2,1,0:T(8,128)(2,1)S(1)}, bf16[1,256,8,256]{3,2,1,0:T(8,128)(2,1)}, u32[]{:S(2)}) copy-start(bf16[1,256,8,256]{3,2,1,0:T(8,128)(2,1)} %basis.1) | copy-start | bytes 3145732
  2.7 20.2 %all-to-all-start = ((bf16[8,272,128]{2,1,0:T(8,128)(2,1)}), bf16[8,272,128]{2,1,0:T(8,128)(2,1)S(1)}, u32[]{:S(2)}, u32[]{:S(2)}) async-start(bf16[8,272,128]{2,1,0:T(8,128)(2,1)} %shard_map.85), calls=%async_computation | async-start | bytes 1114112 | tf_op jit(solution)/shard_map/all_to_all | solution.py:65
  13.6 13.0 %collective-permute-start.1 = (bf16[3,280,256]{2,1,0:T(8,128)(2,1)S(1)}, bf16[3,280,256]{2,1,0:T(8,128)(2,1)S(1)}, u32[]{:S(2)}, u32[]{:S(2)}) collective-permute-start(bf16[3,280,256]{2,1,0:T(8,128)(2,1)S(1)} %get-tuple-element.41), channel_id=1, source_target_pairs={{0,64},{64,0},{128,192},{192,128},{256,320},{320,256},{384,448},{4... | collective-permute-start | bytes 1290248 | tf_op jit(solution)/shard_map/ppermute | solution.py:336
  15.7 10.4 %collective-permute-start = (bf16[3,280,256]{2,1,0:T(8,128)(2,1)S(1)}, bf16[3,280,256]{2,1,0:T(8,128)(2,1)S(1)}, u32[]{:S(2)}, u32[]{:S(2)}) collective-permute-start(bf16[3,280,256]{2,1,0:T(8,128)(2,1)S(1)} %get-tuple-element.42), channel_id=1, source_target_pairs={{64,128},{192,256},{320,384},{128,64},{256,192},{384,320},{65,129}... | collective-permute-start | bytes 1290248 | tf_op jit(solution)/shard_map/ppermute | solution.py:337
  27.3 6.6 %collective-permute-start.3 = (f32[5,16,256]{2,1,0:T(8,128)S(1)}, f32[5,16,256]{2,1,0:T(8,128)S(1)}, u32[]{:S(2)}, u32[]{:S(2)}) collective-permute-start(f32[5,16,256]{2,1,0:T(8,128)S(1)} %get-tuple-element.32.up), channel_id=1, source_target_pairs={{0,1},{1,2},{2,3},{3,4},{4,5},{5,6},{6,7},{7,8},{8,9},{9,10},{10,1... | collective-permute-start | bytes 245768 | tf_op jit(solution)/shard_map/ppermute | solution.py:17
  28.6 5.3 %collective-permute-start.2 = (f32[16,256]{1,0:T(8,128)S(1)}, f32[16,256]{1,0:T(8,128)S(1)}, u32[]{:S(2)}, u32[]{:S(2)}) collective-permute-start(f32[16,256]{1,0:T(8,128)S(1)} %get-tuple-element.34), channel_id=1, source_target_pairs={{0,2},{1,3},{2,4},{3,5},{4,6},{5,7},{6,8},{7,9},{8,10},{9,11},{10,... | collective-permute-start | bytes 49160 | tf_op jit(solution)/shard_map/ppermute | solution.py:17
  32.6 7.2 %collective-permute-start.4 = (f32[5,16,256]{2,1,0:T(8,128)S(1)}, f32[5,16,256]{2,1,0:T(8,128)S(1)}, u32[]{:S(2)}, u32[]{:S(2)}) collective-permute-start(f32[5,16,256]{2,1,0:T(8,128)S(1)} %get-tuple-element.33.down), channel_id=1, source_target_pairs={{1,0},{2,1},{3,2},{4,3},{5,4},{6,5},{7,6},{8,7},{9,8},{10,9},{11,1... | collective-permute-start | bytes 245768 | tf_op jit(solution)/shard_map/ppermute | solution.py:17
  40.9 23.1 %all-to-all-start.1 = ((f32[64,1,128]{2,1,0:T(1,128)}), f32[64,1,128]{2,1,0:T(1,128)S(1)}, u32[]{:S(2)}, u32[]{:S(2)}) async-start(f32[64,1,128]{2,1,0:T(1,128)} %bitcast.17), calls=%async_computation.1 | async-start | bytes 65536 | tf_op jit(solution)/shard_map/all_to_all | solution.py:65
  53.2 5.0 %collective-permute-start.5 = (f32[4,8,256]{2,1,0:T(8,128)S(1)}, f32[4,8,256]{2,1,0:T(8,128)S(1)}, u32[]{:S(2)}, u32[]{:S(2)}) collective-permute-start(f32[4,8,256]{2,1,0:T(8,128)S(1)} %get-tuple-element.36), channel_id=1, source_target_pairs={{1,0},{2,1},{3,2},{4,3},{5,4},{6,5},{7,6},{8,7},{9,8},{10,9},{11,1... | collective-permute-start | bytes 98312 | tf_op jit(solution)/shard_map/ppermute | solution.py:17
